TPU v7x, 512 devices: a whole 4x8x8 slice. The times are simulated.
512 devices in a mesh: expert: 64 (over y, x, core), tensor: 8 (over z).
Axes of the slice: x: 4, y: 8, z: 8, core: 2. Of those that a mesh axis runs over, the one named last changes fastest.
Arguments:
- tokens: bfloat16 [8192, 2048], P('expert'), may hold values from -6 to 6
- cotangent: bfloat16 [8192, 2048], P('expert'), may hold values from -6 to 6
- expert_ids: int32 [8192, 8], P('expert'), may hold values from 0 to 63, all different within a row; in each aligned block of 128 rows (0 to 127, 128 to 255, ...) at most 20 rows name the same one
- gate_probs: bfloat16 [8192, 8], P('expert'), may hold values from 0.049804688 to 0.5
- w_gate: bfloat16 [64, 2048, 1024], P('expert', None, 'tensor'), may hold values from -0.125 to 0.125
- w_up: bfloat16 [64, 2048, 1024], P('expert', None, 'tensor'), may hold values from -0.125 to 0.125
- w_down: bfloat16 [64, 1024, 2048], P('expert', 'tensor'), may hold values from -0.1875 to 0.1875
Outputs:
- grad_input: bfloat16 [8192, 2048], P('expert', 'tensor')
- grad_gate: bfloat16 [64, 2048, 1024], P('expert', None, 'tensor')
- grad_up: bfloat16 [64, 2048, 1024], P('expert', None, 'tensor')
- grad_down: bfloat16 [64, 1024, 2048], P('expert', 'tensor')
Inputs may be any that keep to these rules, and one draw needn't show every extreme that they name: `expert_ids`: each row names 8 different experts. In the 128 rows of one index of the expert axis no expert is named more than 20 times, a bound that some block reaches.
All inputs are finite; a program needn't handle non-finite values.
Results may differ from a plain program's by a relative error of at most 0.019.
Values may be sent and summed in bfloat16 or wider, within the bound.
A program may use at most 128 MiB of HBM per device.

v0:
```python
import jax
import jax.numpy as jnp
from jax import lax
from jax.sharding import PartitionSpec as P

EXPERTS = 64
CAP = 20


def per_device(tokens, cotangent, expert_ids, gate_probs, w_gate, w_up, w_down):
    tok_rows, width = tokens.shape
    top = expert_ids.shape[1]
    routes = tok_rows * top
    hidden = w_gate.shape[2]
    flat_e = expert_ids.reshape(-1)
    onehot = (flat_e[:, None] == jnp.arange(EXPERTS, dtype=jnp.int32)[None, :]).astype(jnp.int32)
    rank = jnp.sum(jnp.cumsum(onehot, axis=0) * onehot, axis=1) - 1
    slot = flat_e * CAP + rank
    source = (
        jnp.full((EXPERTS * CAP,), routes, jnp.int32)
        .at[slot]
        .set(jnp.arange(routes, dtype=jnp.int32))
    )
    live = source < routes
    safe = jnp.minimum(source, routes - 1)
    row_owner = safe // top
    send_probs = jnp.where(
        live, gate_probs.reshape(-1)[safe], jnp.zeros((), gate_probs.dtype)
    ).reshape(EXPERTS, CAP)
    send_x = jnp.where(live[:, None], tokens[row_owner], jnp.zeros((), tokens.dtype)).reshape(
        EXPERTS, CAP, width
    )
    send_c = jnp.where(live[:, None], cotangent[row_owner], jnp.zeros((), cotangent.dtype)).reshape(
        EXPERTS, CAP, width
    )
    rows_x, rows_c, probs = (
        lax.all_to_all(send_x, "expert", split_axis=0, concat_axis=1, tiled=True),
        lax.all_to_all(send_c, "expert", split_axis=0, concat_axis=1, tiled=True),
        lax.all_to_all(send_probs, "expert", split_axis=0, concat_axis=1, tiled=True),
    )
    joined_w = jnp.concatenate([w_gate, w_up], axis=2)
    prob = probs.astype(jnp.float32)[..., None]
    both = jnp.einsum("erd,edf->erf", rows_x, joined_w, preferred_element_type=jnp.float32)
    gate = both[..., :hidden]
    upper = both[..., hidden:]
    sig = jax.nn.sigmoid(gate)
    act = gate * sig
    dhid = prob * jnp.einsum("erd,efd->erf", rows_c, w_down, preferred_element_type=jnp.float32)
    scaled = (prob * act * upper).astype(jnp.bfloat16)
    dgate = (dhid * upper * sig * (1.0 + gate * (1.0 - sig))).astype(jnp.bfloat16)
    dup = (dhid * act).astype(jnp.bfloat16)
    joined_d = jnp.concatenate([dgate, dup], axis=2)
    grad_down = jnp.einsum(
        "erf,erd->efd", scaled, rows_c, preferred_element_type=jnp.float32
    ).astype(jnp.bfloat16)
    grad_both = jnp.einsum(
        "erd,erf->edf", rows_x, joined_d, preferred_element_type=jnp.float32
    ).astype(jnp.bfloat16)
    grad_gate = grad_both[..., :hidden]
    grad_up = grad_both[..., hidden:]
    rounded = jnp.einsum(
        "erf,edf->erd", joined_d, joined_w, preferred_element_type=jnp.float32
    ).astype(jnp.bfloat16)
    back = lax.all_to_all(rounded, "expert", split_axis=1, concat_axis=0, tiled=True)
    picked = back.reshape(EXPERTS * CAP, width)[slot]
    summed = jnp.sum(picked.reshape(tok_rows, top, width), axis=1, dtype=jnp.float32)
    result = lax.psum_scatter(
        summed.astype(jnp.bfloat16), "tensor", scatter_dimension=1, tiled=True
    )
    return (result, grad_gate, grad_up, grad_down)


def solution(mesh):
    return jax.shard_map(
        per_device,
        mesh=mesh,
        in_specs=(
            P("expert", None),
            P("expert", None),
            P("expert", None),
            P("expert", None),
            P("expert", None, "tensor"),
            P("expert", None, "tensor"),
            P("expert", "tensor", None),
        ),
        out_specs=(
            P("expert", "tensor"),
            P("expert", None, "tensor"),
            P("expert", None, "tensor"),
            P("expert", "tensor", None),
        ),
        check_vma=False,
    )
```

profile of v0, /device:TPU:1, one launch (start us, length us, event | category | flops | bytes accessed | tf_op | source)
XLA Modules:
  0.0 699.9 jit_solution(5695035168401443602)
XLA Ops:
  7.2 0.0 copy-start
  7.2 0.7 broadcast_multiply_fusion
  7.9 0.8 copy.26
  8.7 0.1 eq.29
  8.8 0.1 eq.25
  8.9 0.8 copy.30
  9.7 0.1 reshape.148
  9.8 0.1 copy.25
  9.9 0.1 mul.61
  10.0 18.0 %reduce-window.6 = s32[64,8,128]{2,1,0:T(8,128)S(1)} reduce-window(s32[64,8,128]{2,1,0:T(8,128)S(1)} %fusion.11, s32[]{:T(128)} %constant.16.clone.1), window={size=1x1x128 pad=0_0x0_0x127_0}, to_apply=%region_0.0 | reduce-window | flops 8323072 | bytes 524292 | tf_op jit(solution)/shard_map/reduce-window
  28.0 0.1 slice.32
  28.2 0.1 copy.28
  28.4 0.1 copy.29
  28.5 0.1 broadcast_add_fusion
  28.6 0.1 fusion.10
  28.7 4.3 scatter_custom_fusion
  33.1 8.0 %gather_fusion = bf16[1280]{0:T(1024)(128)(2,1)S(1)} fusion(bf16[1024]{0:T(1024)(128)(2,1)S(1)} %reshape.148, s32[2048]{0:T(1024)S(1)} %get-tuple-element.15), kind=kCustom, calls=%fused_computation | custom fusion | bytes 10240 | tf_op jit(solution)/shard_map/gather | solution.py:28
  41.1 0.7 all_to_all.16
  41.8 11.6 %all-to-all-start = ((bf16[64,1,20]{2,1,0:T(2,128)(2,1)}), bf16[64,1,20]{2,1,0:T(2,128)(2,1)S(1)}, u32[]{:S(2)}, u32[]{:S(2)}) async-start(bf16[64,1,20]{2,1,0:T(2,128)(2,1)} %all_to_all.16), calls=%async_computation | async-start | bytes 65536 | tf_op jit(solution)/shard_map/all_to_all | solution.py:39
  53.4 0.1 broadcast_in_dim.37
  53.5 0.0 copy-done
  53.6 6.1 gather_fusion.2
  59.7 9.0 %gather.20 = bf16[64,20,2048]{2,1,0:T(8,128)(2,1)} reshape(bf16[1280,2048]{1,0:T(8,128)(2,1)} %gather_fusion.2) | data formatting | bytes 10485760 | tf_op jit(solution)/shard_map/gather | solution.py:30
  68.6 6.1 gather_fusion.1
  74.7 8.9 %gather.18 = bf16[64,20,2048]{2,1,0:T(8,128)(2,1)} reshape(bf16[1280,2048]{1,0:T(8,128)(2,1)} %gather_fusion.1) | data formatting | bytes 10485760 | tf_op jit(solution)/shard_map/gather | solution.py:33
  83.6 10.3 %broadcast_select_fusion = (bf16[64,20,2048]{2,1,0:T(8,128)(2,1)}, bf16[64,20,2048]{2,1,0:T(8,128)(2,1)}) fusion(bf16[64,20,2048]{2,1,0:T(8,128)(2,1)} %gather.20, pred[64,20]{1,0:T(8,128)(4,1)S(1)} %broadcast_in_dim.37, bf16[64,20,2048]{2,1,0:T(8,128)(2,1)} %gather.18), kind=kLoop, calls=%fused_computation.7 | loop fusion | flops 5242880 | bytes 20972800 | tf_op jit(solution)/shard_map/jit(_where)/select_n | solution.py:30
  93.9 0.0 all-to-all-done
  93.9 150.0 %all_to_all.41 = bf16[64,20,2048]{2,1,0:T(8,128)(2,1)} all-to-all(bf16[64,20,2048]{2,1,0:T(8,128)(2,1)} %get-tuple-element.10), channel_id=1, replica_groups=mesh['expert'=64,'tensor'=8] {'expert'}, dimensions={0} | all-to-all | bytes 10485760 | tf_op jit(solution)/shard_map/all_to_all | solution.py:37
  243.9 7.2 %all-to-all-start.1 = ((bf16[64,20,2048]{2,1,0:T(8,128)(2,1)}), bf16[64,20,2048]{2,1,0:T(8,128)(2,1)}, u32[]{:S(2)}, u32[]{:S(2)}) async-start(bf16[64,20,2048]{2,1,0:T(8,128)(2,1)} %get-tuple-element.11), calls=%async_computation.1 | async-start | bytes 12582912 | tf_op jit(solution)/shard_map/all_to_all | solution.py:38
  251.1 0.1 convert_reduce_fusion
  251.2 0.1 reshape.157
  251.3 0.0 copy-start.4
  251.3 0.0 copy-start.5
  251.3 9.1 %reshape.151 = bf16[1280,2048]{1,0:T(8,128)(2,1)} reshape(bf16[64,20,2048]{2,1,0:T(8,128)(2,1)} %all_to_all.41) | data formatting | bytes 10485760 | tf_op jit(solution)/shard_map/reshape.24
  260.4 0.0 copy-done.4
  260.4 4.1 convolution_bitcast_fusion
  264.5 0.0 copy-start.3
  264.5 125.4 %all-to-all-done.1 = bf16[64,20,2048]{2,1,0:T(8,128)(2,1)} async-done(((bf16[64,20,2048]{2,1,0:T(8,128)(2,1)}), bf16[64,20,2048]{2,1,0:T(8,128)(2,1)}, u32[]{:S(2)}, u32[]{:S(2)}) %all-to-all-start.1) | async-done | bytes 5242912 | tf_op jit(solution)/shard_map/all_to_all | solution.py:38
  389.9 9.0 %reshape.149 = bf16[1280,2048]{1,0:T(8,128)(2,1)} reshape(bf16[64,20,2048]{2,1,0:T(8,128)(2,1)} %all-to-all-done.1) | data formatting | bytes 10485760 | tf_op jit(solution)/shard_map/reshape.15
  398.9 4.5 multiply_convert_fusion.2
  403.4 0.0 copy-start.8
  403.4 0.0 copy-start.6
  403.4 0.7 copy-done.8
  404.1 1.6 fusion
  405.7 30.6 %copy.39 = bf16[1,1280,2048]{2,0,1:T(2,128)(2,1)} copy(bf16[1,1280,2048]{2,1,0:T(8,128)(2,1)S(1)} %fusion) | data formatting | bytes 10485760 | tf_op jit(solution)/shard_map/convert_element_type | solution.py:63
  436.3 0.0 copy-done.6
  436.3 0.5 broadcast.130
  436.8 32.9 %reduce.5 = bf16[1280,2048]{1,0:T(8,128)(2,1)} reduce(bf16[1280,1,2048]{2,1,0:T(2,128)(2,1)} %bitcast.57, bf16[]{:T(256)} %broadcast.130), dimensions={1}, to_apply=%bitcast.54.reduce_sub_computation | reduce | bytes 10485762
  469.7 12.9 %reshape.210 = bf16[64,2,20480]{2,1,0:T(2,128)(2,1)} reshape(bf16[1280,2048]{1,0:T(8,128)(2,1)} %reduce.5) | data formatting | bytes 10485760
  482.6 8.3 %all-to-all-start.3 = ((bf16[64,2,20480]{2,1,0:T(2,128)(2,1)}), bf16[64,2,20480]{2,1,0:T(2,128)(2,1)}, u32[]{:S(2)}, u32[]{:S(2)}) async-start(bf16[64,2,20480]{2,1,0:T(2,128)(2,1)} %reshape.210), calls=%async_computation.3 | async-start | bytes 10485760 | tf_op jit(solution)/shard_map/all_to_all | solution.py:64
  490.8 0.0 reduce-scatter.2.cloned.1.call-start
  490.9 116.4 %all-to-all-done.3 = bf16[64,2,20480]{2,1,0:T(2,128)(2,1)} async-done(((bf16[64,2,20480]{2,1,0:T(2,128)(2,1)}), bf16[64,2,20480]{2,1,0:T(2,128)(2,1)}, u32[]{:S(2)}, u32[]{:S(2)}) %all-to-all-start.3) | async-done | bytes 5242912 | tf_op jit(solution)/shard_map/all_to_all | solution.py:64
  607.3 20.6 %reshape.211 = bf16[1280,1,2048]{2,1,0:T(2,128)(2,1)} reshape(bf16[64,2,20480]{2,1,0:T(2,128)(2,1)} %all-to-all-done.3) | data formatting | bytes 10485760
  628.0 9.6 %copy.38 = bf16[1,1280,2048]{2,1,0:T(8,128)(2,1)} copy(bf16[1,1280,2048]{2,0,1:T(2,128)(2,1)} %bitcast.58) | data formatting | bytes 10485760
  637.6 12.0 %gather_fusion.3 = bf16[1024,2048]{1,0:T(8,128)(2,1)} fusion(bf16[1280,2048]{1,0:T(8,128)(2,1)} %bitcast.56, s32[1024]{0:T(1024)S(1)} %broadcast_clamp_fusion), kind=kCustom, calls=%fused_computation.3 | custom fusion | bytes 8392704 | tf_op jit(solution)/shard_map/gather | solution.py:65
  649.6 6.0 bitcast_reduce_fusion
  655.6 0.0 reduce-scatter.2.cloned.1.call-update
  655.6 0.0 slice-start.1
  655.6 0.0 copy-start.1
  655.6 4.4 fusion.3
  660.0 0.0 slice-done.1
  660.0 2.6 fusion.1
  662.6 1.0 fusion.21
  663.6 29.4 %reduce-scatter.2.cloned.1.call-done = bf16[128,256]{1,0:T(8,128)(2,1)} async-done(((bf16[128,2048]{1,0:T(8,128)(2,1)}), bf16[128,256]{1,0:T(8,128)(2,1)}) %reduce-scatter.2.cloned.1.call-update) | async-done | bytes 65552 | tf_op jit(solution)/shard_map/reduce_scatter | solution.py:67
  (20 shorter events, 0.1 us)
Async XLA Ops:
  7.2 46.4 %copy-start = (bf16[128,2048]{1,0:T(8,128)(2,1)S(1)}, bf16[128,2048]{1,0:T(8,128)(2,1)}, u32[]{:S(2)}) copy-start(bf16[128,2048]{1,0:T(8,128)(2,1)} %param.7) | copy-start | bytes 1572868
  41.8 52.1 %all-to-all-start = ((bf16[64,1,20]{2,1,0:T(2,128)(2,1)}), bf16[64,1,20]{2,1,0:T(2,128)(2,1)S(1)}, u32[]{:S(2)}, u32[]{:S(2)}) async-start(bf16[64,1,20]{2,1,0:T(2,128)(2,1)} %all_to_all.16), calls=%async_computation | async-start | bytes 65536 | tf_op jit(solution)/shard_map/all_to_all | solution.py:39
  59.7 9.0 %copy-start.2 = (bf16[128,2048]{1,0:T(8,128)(2,1)S(1)}, bf16[128,2048]{1,0:T(8,128)(2,1)}, u32[]{:S(2)}) copy-start(bf16[128,2048]{1,0:T(8,128)(2,1)} %param.8) | copy-start | bytes 1572868
  243.9 146.1 %all-to-all-start.1 = ((bf16[64,20,2048]{2,1,0:T(8,128)(2,1)}), bf16[64,20,2048]{2,1,0:T(8,128)(2,1)}, u32[]{:S(2)}, u32[]{:S(2)}) async-start(bf16[64,20,2048]{2,1,0:T(8,128)(2,1)} %get-tuple-element.11), calls=%async_computation.1 | async-start | bytes 12582912 | tf_op jit(solution)/shard_map/all_to_all | solution.py:38
  251.3 9.1 %copy-start.4 = (bf16[1,2048,128]{2,1,0:T(8,128)(2,1)S(1)}, bf16[1,2048,128]{2,1,0:T(8,128)(2,1)}, u32[]{:S(2)}) copy-start(bf16[1,2048,128]{2,1,0:T(8,128)(2,1)} %param.12) | copy-start | bytes 1572868
  251.3 9.1 %copy-start.5 = (bf16[1,2048,128]{2,1,0:T(8,128)(2,1)S(1)}, bf16[1,2048,128]{2,1,0:T(8,128)(2,1)}, u32[]{:S(2)}) copy-start(bf16[1,2048,128]{2,1,0:T(8,128)(2,1)} %param.11) | copy-start | bytes 1572868
  264.5 134.4 %copy-start.3 = (bf16[1,128,2048]{2,1,0:T(8,128)(2,1)S(1)}, bf16[1,128,2048]{2,1,0:T(8,128)(2,1)}, u32[]{:S(2)}) copy-start(bf16[1,128,2048]{2,1,0:T(8,128)(2,1)} %param.13) | copy-start | bytes 1572868
  403.4 0.7 copy-start.8
  403.4 32.9 %copy-start.6 = (bf16[1,1280,128]{1,2,0:T(8,128)(2,1)}, bf16[1,1280,128]{1,2,0:T(8,128)(2,1)S(1)}, u32[]{:S(2)}) copy-start(bf16[1,1280,128]{1,2,0:T(8,128)(2,1)S(1)} %get-tuple-element.6) | copy-start | bytes 983044
  482.6 124.8 %all-to-all-start.3 = ((bf16[64,2,20480]{2,1,0:T(2,128)(2,1)}), bf16[64,2,20480]{2,1,0:T(2,128)(2,1)}, u32[]{:S(2)}, u32[]{:S(2)}) async-start(bf16[64,2,20480]{2,1,0:T(2,128)(2,1)} %reshape.210), calls=%async_computation.3 | async-start | bytes 10485760 | tf_op jit(solution)/shard_map/all_to_all | solution.py:64
  490.8 202.2 %reduce-scatter.2.cloned.1.call-start = ((), (), s32[]{:S(2)}) async-start(), calls=%async_computation.5 | async-start | bytes 589824 | tf_op jit(solution)/shard_map/reduce_scatter | solution.py:67
  649.6 10.4 %slice-start = ((s8[5242880]{0:T(1024)(128)(4,1)}), s8[1048576]{0:T(1024)(128)(4,1)S(1)}, s32[]{:S(2)}) async-start(s8[5242880]{0:T(1024)(128)(4,1)} %bitcast.59), calls=%async_computation.6 | async-start | bytes 2097152
  655.6 4.4 copy-start.7
  655.6 4.4 slice-start.1
  655.6 37.5 %copy-start.1 = (bf16[128,2048]{1,0:T(8,128)(2,1)S(1)}, bf16[128,2048]{1,0:T(8,128)(2,1)}, u32[]{:S(2)}) copy-start(bf16[128,2048]{1,0:T(8,128)(2,1)} %param.7) | copy-start | bytes 1572868
Sparse Core Ops, SparseCore 0:
  655.7 37.3 reduce-scatter.1
where the time goes:
time: 706 us; the launch traced here: 700 us
  waiting for transfers between devices  271 us (38%)
  local copies, waits for them, and re-layouts  152 us (22%)
  blocking collectives  150 us (21%)
  other arithmetic  68.2 us (10%)
  starting transfers between devices  27.2 us (4%)
  matrix products  17.1 us (2%)
  between operations  14.3 us (2%)
    all_to_all x1, blocking collectives, per_device(): lax.all_to_all(send_x, 'expert', split_axis=0, concat_axis=1, tiled=True)  150 us
    all_to_all x1, waiting for transfers between devices, per_device(): lax.all_to_all(send_c, 'expert', split_axis=0, concat_axis=1, tiled=True)  125 us
    all_to_all x1, waiting for transfers between devices, per_device(): lax.all_to_all(rounded, 'expert', split_axis=1, concat_axis=0, tiled=True)  116 us
    unnamed x28, local copies, waits for them, and re-layouts  46 us
    unnamed x2, other arithmetic  32.9 us
    convert_element_type x1, local copies, waits for them, and re-layouts, per_device(): rounded = jnp.einsum('erf,edf->erd', joined_d, joined_w, preferred_elemen...  30.6 us
    reduce_scatter x1, waiting for transfers between devices, per_device(): lax.psum_scatter(summed.astype(jnp.bfloat16), 'tensor', scatter_dimension...  29.4 us
    another operation x3, other arithmetic  18.2 us
  transfers between devices with their start and end apart: 4, of which 3 were waited for; matrix products, arithmetic and copies ran while one was open for 9% of the time, Pallas kernels for 0%

commit v1 on v0

v1 whole, which is shorter than its diff:
```python
import functools

import jax
import jax.numpy as jnp
import ml_dtypes
import numpy as np
from jax import lax
from jax.experimental import pallas as pl
from jax.experimental.pallas import tpu as pltpu
from jax.sharding import PartitionSpec as P

MESH = pl.DeviceIdType.MESH
BF = jnp.bfloat16
F32 = jnp.float32
CAP = 20
SIDE = 4
LANES = 128
PART = 256
OUT = 4 * CAP
BACK = 48


def dot(a, b):
    return jnp.dot(a, b, preferred_element_type=F32)


def dot_t(a, b):
    return lax.dot_general(a, b, (((1,), (1,)), ((), ())), preferred_element_type=F32)


def t_dot(a, b):
    return lax.dot_general(a, b, (((0,), (0,)), ((), ())), preferred_element_type=F32)


def kernel(
    ne, nt, side, gp,
    ids_ref, idst_ref, probst_ref, tok_ref, cot_ref, wg_ref, wu_ref, wd_ref,
    perm_ref, back_ref, expand_ref, phase_ref,
    gi_ref, gg_ref, gu_ref, gd_ref,
    key_ref, pr_ref, rhs_ref, sel_ref, send_ref, recv_ref, g_ref, w_ref, d_ref, sc_ref,
    rs_send, rs_recv, ret_send, ret_recv, lo_ref, hi_ref,
    a2a_s, a2a_r, ag_s, ag_r, rs_s, rs_r, ret_s, ret_r,
):
    wide = 2 * side
    ny = ne // wide
    half = nt // 2
    rows = wide * CAP
    tokens = tok_ref.shape[0]
    ei, ti = lax.axis_index("expert"), lax.axis_index("tensor")
    yy, xx, core = ei // wide, lax.rem(ei // 2, side), lax.rem(ei, 2)
    right, left = lax.rem(ti + 1, nt), lax.rem(ti + nt - 1, nt)
    opp = lax.rem(ti + half, nt)

    def away(c):
        h, odd = (c + 1) // 2, lax.rem(c, 2)
        return odd * h + (1 - odd) * (ny - h)

    def row_to(c):
        return lax.rem(yy + 2 * ny - away(c), ny)

    def peer_to(c, s):
        dx, dc = s // 2, s % 2
        return row_to(c) * wide + lax.rem(xx + side - dx, side) * 2 + lax.rem(core + dc, 2)

    def peer_from(c, s):
        dx, dc = s // 2, s % 2
        return (
            lax.rem(yy + away(c), ny) * wide
            + lax.rem(xx + dx, side) * 2
            + lax.rem(core + dc, 2)
        )

    def others(act):
        for s in range(1, wide):
            act(0, s)

        @pl.loop(1, ny)
        def _(c):
            for s in range(wide):
                act(c, s)

    bar = pltpu.get_barrier_semaphore()
    others(
        lambda c, s: pl.semaphore_signal(
            bar, inc=1, device_id=(peer_to(c, s), ti), device_id_type=MESH
        )
    )
    for z in (right, left):
        pl.semaphore_signal(bar, inc=1, device_id=(ei, z), device_id_type=MESH)

    hits = jnp.zeros((ne, tokens), F32)
    prob = jnp.zeros((ne, tokens), F32)
    experts = lax.broadcasted_iota(jnp.int32, (ne, tokens), 0)
    for k in range(idst_ref.shape[0]):
        hit = idst_ref[k : k + 1, :] == experts
        hits = jnp.where(hit, 1.0, hits)
        prob = jnp.where(hit, probst_ref[k : k + 1, :], prob)
    r0 = lax.broadcasted_iota(jnp.int32, (tokens, tokens), 0)
    r1 = lax.broadcasted_iota(jnp.int32, (tokens, tokens), 1)
    before = jnp.where(r0 < r1, 1.0, 0.0).astype(BF)
    key_ref[...] = jnp.where(hits > 0.0, dot(hits.astype(BF), before), -1000.0)
    pr_ref[...] = prob

    for j in range(2):
        for m, start in enumerate((ti, opp)):
            at = pl.multiple_of(start * PART + j * LANES, LANES)
            cols = slice(m * LANES, (m + 1) * LANES)
            rhs_ref[j * tokens : (j + 1) * tokens, cols] = tok_ref[:, pl.ds(at, LANES)]
            rhs_ref[(2 + j) * tokens : (3 + j) * tokens, cols] = cot_ref[:, pl.ds(at, LANES)]

    def send_copy(c, s):
        to = peer_to(c, s)
        return pltpu.make_async_remote_copy(
            src_ref=send_ref.at[pl.ds(pl.multiple_of(to * OUT, OUT), OUT)],
            dst_ref=recv_ref.at[pl.ds(pl.multiple_of((c * wide + s) * OUT, OUT), OUT)],
            send_sem=a2a_s,
            recv_sem=a2a_r.at[c],
            device_id=(to, ti),
            device_id_type=MESH,
        )

    def pack(c):
        first = row_to(c) * wide
        keys = key_ref[pl.ds(pl.multiple_of(first, wide), wide), :]
        probs = pr_ref[pl.ds(pl.multiple_of(first, wide), wide), :]
        place = lax.broadcasted_iota(jnp.int32, (OUT, tokens), 0).astype(F32)
        for i in range(wide):
            key = jnp.broadcast_to(keys[i : i + 1, :], (OUT, tokens))
            share = jnp.broadcast_to(probs[i : i + 1, :], (OUT, tokens))
            for j in range(4):
                value = 1.0 if j < 2 else share
                sel_ref[i * OUT : (i + 1) * OUT, j * tokens : (j + 1) * tokens] = jnp.where(
                    place - float(CAP * j) == key, value, 0.0
                ).astype(BF)
        at = pl.ds(pl.multiple_of(first * OUT, OUT), wide * OUT)
        send_ref[at, :] = dot(sel_ref[...], rhs_ref[...]).astype(BF)

    pack(0)
    own = pltpu.make_async_copy(
        send_ref.at[pl.ds(pl.multiple_of(ei * OUT, OUT), OUT)],
        recv_ref.at[pl.ds(0, OUT)],
        a2a_r.at[0],
    )
    own.start()
    pl.semaphore_wait(bar, ne + 1)
    for s in range(1, wide):
        send_copy(0, s).start()

    @pl.loop(1, ny)
    def _(c):
        pack(c)
        for s in range(wide):
            send_copy(c, s).start()

    w_ref[:, :LANES] = wg_ref[...]
    w_ref[:, LANES:] = wu_ref[...]

    def block(c):
        return pl.ds(pl.multiple_of(c * rows, rows), rows)

    def ag_copy(c, s, way):
        unit = lax.rem(ti + nt - s, nt) if way == 0 else lax.rem(ti + s, nt)
        ref = g_ref.at[unit, block(c)]
        return pltpu.make_async_remote_copy(
            src_ref=ref,
            dst_ref=ref,
            send_sem=ag_s.at[way, s],
            recv_sem=ag_r.at[way, s, c],
            device_id=(ei, right if way == 0 else left),
            device_id_type=MESH,
        )

    def arrive(c):
        got = recv_ref.at[pl.ds(pl.multiple_of(c * wide * OUT, OUT), wide * OUT)]
        pltpu.make_async_copy(got, got, a2a_r.at[c]).wait()
        for g in range(wide // gp):
            at = pl.multiple_of((c * wide + g * gp) * OUT, OUT)
            out = dot(perm_ref[...], recv_ref[pl.ds(at, gp * OUT), :]).astype(BF)
            to = pl.ds(pl.multiple_of(c * rows + g * gp * CAP, gp * CAP), gp * CAP)
            for j in range(4):
                piece = out[j * gp * CAP : (j + 1) * gp * CAP, :]
                g_ref[ti, to, j * LANES : (j + 1) * LANES] = piece[:, :LANES]
                g_ref[opp, to, j * LANES : (j + 1) * LANES] = piece[:, LANES:]
        for way in range(2):
            ag_copy(c, 0, way).start()

    def ag_wait(c, s):
        for way in range(2):
            unit = lax.rem(ti + nt - s - 1, nt) if way == 0 else lax.rem(ti + s + 1, nt)
            ref = g_ref.at[unit, block(c)]
            pltpu.make_async_copy(ref, ref, ag_r.at[way, s, c]).wait()

    def forward(s, c):
        ag_wait(c, s - 1)
        for way in range(2):
            ag_copy(c, s, way).start()

    def piece_of(c, target):
        at = pl.ds(pl.multiple_of(target * PART, PART), PART)
        return dot_t(d_ref[block(c), :], w_ref[at, :])

    def rs_rows(c, k, way):
        if k > 0:
            return block(c)
        return pl.ds(pl.multiple_of(c * rows + way * (rows // 2), rows // 2), rows // 2)

    def rs_copy(c, k, way):
        at = rs_rows(c, k, way)
        return pltpu.make_async_remote_copy(
            src_ref=rs_send.at[0 if k == 0 else way, k, at],
            dst_ref=rs_recv.at[way, k, at],
            send_sem=rs_s.at[way, k],
            recv_sem=rs_r.at[way, k, c],
            device_id=(ei, right if way == 0 else left),
            device_id_type=MESH,
        )

    def rs_wait(c, k, way):
        ref = rs_recv.at[way, k, rs_rows(c, k, way)]
        pltpu.make_async_copy(ref, ref, rs_r.at[way, k, c]).wait()

    def middle(c):
        ag_wait(c, half - 2)
        at = block(c)
        both = jnp.zeros((rows, 2 * LANES), F32)
        dhid = jnp.zeros((rows, LANES), F32)
        for u in range(nt):
            cols = slice(u * PART, (u + 1) * PART)
            both = both + dot(g_ref[u, at, :PART], w_ref[cols, :])
            dhid = dhid + dot_t(g_ref[u, at, PART:], wd_ref[:, cols])
        gate, upper = both[:, :LANES], both[:, LANES:]
        sig = 1.0 / (1.0 + jnp.exp(-gate))
        act = gate * sig
        sc_ref[at, :] = (act * upper).astype(BF)
        d_ref[at, :LANES] = (dhid * upper * sig * (1.0 + gate * (1.0 - sig))).astype(BF)
        d_ref[at, LANES:] = (dhid * act).astype(BF)
        rs_send[0, 0, at, :] = piece_of(c, opp).astype(BF)
        for way in range(2):
            rs_copy(c, 0, way).start()

    def add(k, c):
        for way in range(2):
            hop = half - k
            target = lax.rem(ti + hop, nt) if way == 0 else lax.rem(ti + nt - hop, nt)
            piece = piece_of(c, target)
            rs_wait(c, k - 1, way)
            if k > 1:
                got = rs_recv[way, k - 1, block(c), :].astype(F32)
                rs_send[way, k, block(c), :] = (piece + got).astype(BF)
            else:
                for part in range(2):
                    at = rs_rows(c, 0, part)
                    here = piece[part * (rows // 2) : (part + 1) * (rows // 2), :]
                    if part == way:
                        here = here + rs_recv[way, 0, at, :].astype(F32)
                    rs_send[way, k, at, :] = here.astype(BF)
            rs_copy(c, k, way).start()

    def back_copy(c, s):
        return pltpu.make_async_remote_copy(
            src_ref=ret_send.at[pl.ds(pl.multiple_of((c * wide + s) * BACK, BACK), BACK)],
            dst_ref=ret_recv.at[pl.ds(pl.multiple_of(ei * BACK, BACK), BACK)],
            send_sem=ret_s,
            recv_sem=ret_r.at[c],
            device_id=(peer_from(c, s), ti),
            device_id_type=MESH,
        )

    def finish(c):
        piece = piece_of(c, ti)
        for way in range(2):
            rs_wait(c, half - 1, way)
            piece = piece + rs_recv[way, half - 1, block(c), :].astype(F32)
        whole = piece.astype(BF)
        at = pl.ds(pl.multiple_of(c * wide * BACK, BACK), wide * BACK)
        ret_send[at, :] = (
            dot(back_ref[0], whole[:, :LANES]) + dot(back_ref[1], whole[:, LANES:])
        ).astype(BF)

        @pl.when(c == 0)
        def _():
            pltpu.make_async_copy(
                ret_send.at[pl.ds(0, BACK)],
                ret_recv.at[pl.ds(pl.multiple_of(ei * BACK, BACK), BACK)],
                ret_r.at[c],
            ).start()

        @pl.when(c != 0)
        def _():
            back_copy(c, 0).start()

        for s in range(1, wide):
            back_copy(c, s).start()

    def weight_grads(u):
        at = pl.ds(pl.multiple_of(u * PART, PART), PART)
        both = t_dot(g_ref[u, :, :PART], d_ref[...]).astype(BF)
        gg_ref[at, :] = both[:, :LANES]
        gu_ref[at, :] = both[:, LANES:]
        gd_ref[:, at] = t_dot(sc_ref[...], g_ref[u, :, PART:]).astype(BF)

    stages = [arrive]
    stages += [functools.partial(forward, s) for s in range(1, half - 1)]
    stages += [middle]
    stages += [functools.partial(add, k) for k in range(1, half)]
    stages += [finish]

    hits_n = jnp.zeros((tokens, ne), F32)
    experts_n = lax.broadcasted_iota(jnp.int32, (tokens, ne), 1)
    for k in range(ids_ref.shape[1]):
        hits_n = jnp.where(ids_ref[:, k : k + 1] == experts_n, 1.0, hits_n)
    after = jnp.where(r1 < r0, 1.0, 0.0).astype(BF)
    key_n = jnp.where(hits_n > 0.0, dot(after, hits_n.astype(BF)), 200.0).astype(BF)
    tile = min(ne * BACK, 512)
    for n in range(0, ne * BACK, tile):
        want = dot(key_n, expand_ref[:, n : n + tile])
        phase = phase_ref[:, n : n + tile]
        lo_ref[:, n : n + tile] = jnp.where(want == phase, 1.0, 0.0).astype(BF)
        hi_ref[:, n : n + tile] = jnp.where(want + float(CAP) == phase, 1.0, 0.0).astype(BF)

    last = ny + half - 1
    each = nt // half

    @pl.loop(0, ny + len(stages) - 1)
    def _(turn):
        for i, stage in enumerate(stages):
            c = turn - i
            pl.when(jnp.logical_and(c >= 0, c < ny))(functools.partial(stage, c))

        @pl.when(turn >= last)
        def _():
            for i in range(each):
                weight_grads((turn - last) * each + i)

    @pl.loop(0, ny)
    def _(c):
        got = ret_recv.at[pl.ds(pl.multiple_of(c * wide * BACK, BACK), wide * BACK)]
        pltpu.make_async_copy(got, got, ret_r.at[c]).wait()

    gi_ref[:, :LANES] = dot(lo_ref[...], ret_recv[...]).astype(BF)
    gi_ref[:, LANES:] = dot(hi_ref[...], ret_recv[...]).astype(BF)

    sent = send_ref.at[pl.ds(0, (ne - 1) * OUT)]
    pltpu.make_async_copy(sent, sent, a2a_s).wait()
    sent = ret_send.at[pl.ds(0, (ne - 1) * BACK)]
    pltpu.make_async_copy(sent, sent, ret_s).wait()
    for way in range(2):
        for s in range(half - 1):
            pltpu.make_async_copy(g_ref.at[0], g_ref.at[0], ag_s.at[way, s]).wait()
        for k in range(half):
            sent = rs_send.at[0, 0]
            if k == 0:
                sent = rs_send.at[0, 0, pl.ds(0, ny * (rows // 2))]
            pltpu.make_async_copy(sent, sent, rs_s.at[way, k]).wait()


def tables(ne, side):
    wide = 2 * side
    gp = min(4, wide)
    perm = np.zeros((gp * OUT, gp * OUT), np.float32)
    for j in range(4):
        for s in range(gp):
            for r in range(CAP):
                perm[j * gp * CAP + s * CAP + r, s * OUT + j * CAP + r] = 1.0
    back = np.zeros((2, wide * BACK, wide * CAP), np.float32)
    for s in range(wide):
        for r in range(CAP):
            for m in range(2):
                back[m, s * BACK + m * CAP + r, s * CAP + r] = 1.0
    expand = np.kron(np.eye(ne, dtype=np.float32), np.ones((1, BACK), np.float32))
    phase = np.tile(np.arange(BACK, dtype=np.float32), ne)[None, :]
    half = ml_dtypes.bfloat16
    return gp, perm.astype(half), back.astype(half), expand.astype(half), phase


def solution(mesh):
    ne, nt = mesh.shape["expert"], mesh.shape["tensor"]
    side = SIDE
    wide = 2 * side
    ny, half = ne // wide, nt // 2
    rows = ne * CAP
    gp, perm, back, expand, phase = tables(ne, side)

    def step(tokens, cotangent, expert_ids, gate_probs, w_gate, w_up, w_down):
        owned, width = tokens.shape
        vmem = pl.BlockSpec(memory_space=pltpu.VMEM)
        dma = pltpu.SemaphoreType.DMA
        gi, gg, gu, gd = pl.pallas_call(
            functools.partial(kernel, ne, nt, side, gp),
            out_shape=(
                jax.ShapeDtypeStruct((owned, PART), BF),
                jax.ShapeDtypeStruct((width, LANES), BF),
                jax.ShapeDtypeStruct((width, LANES), BF),
                jax.ShapeDtypeStruct((LANES, width), BF),
            ),
            in_specs=[vmem] * 12,
            out_specs=(vmem,) * 4,
            scratch_shapes=[
                pltpu.VMEM((ne, owned), F32),
                pltpu.VMEM((ne, owned), F32),
                pltpu.VMEM((4 * owned, 2 * LANES), BF),
                pltpu.VMEM((wide * OUT, 4 * owned), BF),
                pltpu.VMEM((ne * OUT, 2 * LANES), BF),
                pltpu.VMEM((ne * OUT, 2 * LANES), BF),
                pltpu.VMEM((nt, rows, 2 * PART), BF),
                pltpu.VMEM((width, 2 * LANES), BF),
                pltpu.VMEM((rows, 2 * LANES), BF),
                pltpu.VMEM((rows, LANES), BF),
                pltpu.VMEM((2, half, rows, PART), BF),
                pltpu.VMEM((2, half, rows, PART), BF),
                pltpu.VMEM((ne * BACK, LANES), BF),
                pltpu.VMEM((ne * BACK, LANES), BF),
                pltpu.VMEM((owned, ne * BACK), BF),
                pltpu.VMEM((owned, ne * BACK), BF),
                dma,
                dma((ny,)),
                dma((2, half - 1)),
                dma((2, half - 1, ny)),
                dma((2, half)),
                dma((2, half, ny)),
                dma,
                dma((ny,)),
            ],
            compiler_params=pltpu.CompilerParams(
                collective_id=0, has_side_effects=True, vmem_limit_bytes=56 * 1024 * 1024
            ),
        )(
            expert_ids,
            expert_ids.T,
            gate_probs.T.astype(F32),
            tokens,
            cotangent,
            w_gate[0],
            w_up[0],
            w_down[0],
            jnp.asarray(perm),
            jnp.asarray(back),
            jnp.asarray(expand),
            jnp.asarray(phase),
        )
        return gi, gg[None], gu[None], gd[None]

    return jax.shard_map(
        step,
        mesh=mesh,
        in_specs=(
            P("expert", None),
            P("expert", None),
            P("expert", None),
            P("expert", None),
            P("expert", None, "tensor"),
            P("expert", None, "tensor"),
            P("expert", "tensor", None),
        ),
        out_specs=(
            P("expert", "tensor"),
            P("expert", None, "tensor"),
            P("expert", None, "tensor"),
            P("expert", "tensor", None),
        ),
        check_vma=False,
    )
```

time: 706 us -> 190 us (0.27)
  waiting for transfers between devices: 271 us -> 0 us
  Pallas kernels: 0 us -> 182 us
  blocking collectives: 150 us -> 0 us
  local copies, waits for them, and re-layouts: 152 us -> 6.82 us
  other arithmetic: 68.2 us -> 0.59 us
  starting transfers between devices: 27.2 us -> 0 us
  matrix products: 17.1 us -> 0 us
  between operations: 14.3 us -> 0.66 us
    all_to_all x3 -> x0, waiting for transfers between devices: 242 us -> none  [the longest x1 125 us: per_device(): lax.all_to_all(send_c, 'expert', split_axis=0, concat_axis=1, tiled=True)]
    pallas_call x0 -> x1, Pallas kernels: none -> 182 us  [step(): pl.pallas_call(functools.partial(kernel, ne, nt, side, gp), out_shape=(ja...]
    all_to_all x1 -> x0, blocking collectives: 150 us -> none  [per_device(): lax.all_to_all(send_x, 'expert', split_axis=0, concat_axis=1, tiled=True)]
    gather x6 -> x0, local copies, waits for them, and re-layouts: 50 us -> none  [the longest x2 15.1 us: per_device(): tokens[row_owner]]
    unnamed x28 -> x13, local copies, waits for them, and re-layouts: 46 us -> 6.82 us
    unnamed x2 -> x0, other arithmetic: 32.9 us -> none
    convert_element_type x2 -> x0, local copies, waits for them, and re-layouts: 30.7 us -> none  [the longest x1 30.6 us: per_device(): rounded = jnp.einsum('erf,edf->erd', joined_d, joined_w, preferred_elemen...]
    reduce_scatter x1 -> x0, waiting for transfers between devices: 29.4 us -> none  [per_device(): lax.psum_scatter(summed.astype(jnp.bfloat16), 'tensor', scatter_dimension...]
  transfers between devices with their start and end apart: 4 -> 0, of which waited for: 3 -> 0; matrix products, arithmetic and copies ran while one was open for 9% -> 0% of each run, Pallas kernels for 0% -> 0%
where the time goes in v1:
time: 190 us
  Pallas kernels  182 us (96%)
  local copies, waits for them, and re-layouts  6.82 us (4%)
    pallas_call x1, Pallas kernels, step(): pl.pallas_call(functools.partial(kernel, ne, nt, side, gp), out_shape=(ja...  182 us
    unnamed x13, local copies, waits for them, and re-layouts  6.82 us

profile of v1, /device:TPU:1, one launch (start us, length us, event | category | flops | bytes accessed | tf_op | source)
XLA Modules:
  0.0 189.6 jit_solution(2956119314600543076)
XLA Ops:
  0.6 0.0 copy-start.3
  0.6 0.0 copy-start.2
  0.7 0.7 copy-done.3
  1.3 0.6 convert_bitcast_fusion.probst_ref
  1.9 0.0 copy-done.2
  1.9 0.7 copy.15.ids_ref
  2.6 181.6 %shard_map.138 = (bf16[128,256]{1,0:T(8,128)(2,1)}, bf16[2048,128]{1,0:T(8,128)(2,1)}, bf16[2048,128]{1,0:T(8,128)(2,1)}, bf16[128,2048]{1,0:T(8,128)(2,1)}) custom-call(s32[128,8]{1,0:T(8,128)} %copy.15.ids_ref, s32[8,128]{1,0:T(8,128)} %bitcast.15, f32[8,128]{1,0:T(8,128)} %convert_bitcast_fusion.probst_ref, bf16[128,2048]{1,0:T(8,128)(2,1)} %tok_ref.1, ...), custom_call_target="tpu_custom_call" | custom-call | tf_op jit(solution)/shard_map/pallas_call | solution.py:388
  184.2 1.5 copy.20
  185.7 0.0 copy-start.1
  185.7 1.9 %copy.21 = bf16[1,2048,128]{2,1,0:T(8,128)(2,1)} copy(bf16[1,2048,128]{2,1,0:T(8,128)(2,1)} %bitcast.11) | data formatting | bytes 1048576
  187.6 0.0 copy-done.1
  187.6 0.0 copy-start
  187.6 0.8 copy.22
  188.4 0.4 copy-done
  188.8 0.8 copy.23
Async XLA Ops:
  0.6 0.7 copy-start.3
  0.6 1.3 copy-start.2
  185.7 1.9 %copy-start.1 = (bf16[2048,128]{1,0:T(8,128)(2,1)S(1)}, bf16[2048,128]{1,0:T(8,128)(2,1)}, u32[]{:S(2)}) copy-start(bf16[2048,128]{1,0:T(8,128)(2,1)} %get-tuple-element.10) | copy-start | bytes 1572868
  187.6 1.2 copy-start

commit v2 on v1

--- a/solution.py
+++ b/solution.py
@@ -18,6 +18,12 @@
 PART = 256
 OUT = 4 * CAP
 BACK = 48
+AHEAD = 1
+LAG = 1
+
+
+def ring_chunks(ny):
+    return ny - 2 if ny > 4 else ny - 1
 
 
 def dot(a, b):
@@ -34,17 +40,18 @@
 
 def kernel(
     ne, nt, side, gp,
-    ids_ref, idst_ref, probst_ref, tok_ref, cot_ref, wg_ref, wu_ref, wd_ref,
+    idst_ref, probst_ref, tok_ref, cot_ref, wg_ref, wu_ref, wd_ref,
     perm_ref, back_ref, expand_ref, phase_ref,
     gi_ref, gg_ref, gu_ref, gd_ref,
-    key_ref, pr_ref, rhs_ref, sel_ref, send_ref, recv_ref, g_ref, w_ref, d_ref, sc_ref,
+    key_ref, pr_ref, rhs_ref, all_ref, sel_ref, send_ref, recv_ref, nsend_ref, nrecv_ref, g_ref, w_ref, d_ref, sc_ref,
     rs_send, rs_recv, ret_send, ret_recv, lo_ref, hi_ref,
-    a2a_s, a2a_r, ag_s, ag_r, rs_s, rs_r, ret_s, ret_r,
+    a2a_s, near_s, a2a_r, ag_s, ag_r, rs_s, rs_r, ret_s, ret_r,
 ):
     wide = 2 * side
     ny = ne // wide
     half = nt // 2
     rows = wide * CAP
+    ring = ring_chunks(ny)
     tokens = tok_ref.shape[0]
     ei, ti = lax.axis_index("expert"), lax.axis_index("tensor")
     yy, xx, core = ei // wide, lax.rem(ei // 2, side), lax.rem(ei, 2)
@@ -52,6 +59,7 @@
     opp = lax.rem(ti + half, nt)
 
     def away(c):
+        c = (lax.rem(c + 1, ny - 1) + 1) * jnp.minimum(c, 1)
         h, odd = (c + 1) // 2, lax.rem(c, 2)
         return odd * h + (1 - odd) * (ny - h)
 
@@ -59,17 +67,20 @@
         return lax.rem(yy + 2 * ny - away(c), ny)
 
     def peer_to(c, s):
-        dx, dc = s // 2, s % 2
+        dx, dc = s // 2, lax.rem(s, 2)
         return row_to(c) * wide + lax.rem(xx + side - dx, side) * 2 + lax.rem(core + dc, 2)
 
     def peer_from(c, s):
-        dx, dc = s // 2, s % 2
+        dx, dc = s // 2, lax.rem(s, 2)
         return (
             lax.rem(yy + away(c), ny) * wide
             + lax.rem(xx + dx, side) * 2
             + lax.rem(core + dc, 2)
         )
 
+    def turned(i):
+        return lax.rem(i + core * (wide // 2), wide)
+
     def others(act):
         for s in range(1, wide):
             act(0, s)
@@ -91,10 +102,11 @@
     hits = jnp.zeros((ne, tokens), F32)
     prob = jnp.zeros((ne, tokens), F32)
     experts = lax.broadcasted_iota(jnp.int32, (ne, tokens), 0)
+    given = probst_ref[...].astype(F32)
     for k in range(idst_ref.shape[0]):
         hit = idst_ref[k : k + 1, :] == experts
         hits = jnp.where(hit, 1.0, hits)
-        prob = jnp.where(hit, probst_ref[k : k + 1, :], prob)
+        prob = jnp.where(hit, given[k : k + 1, :], prob)
     r0 = lax.broadcasted_iota(jnp.int32, (tokens, tokens), 0)
     r1 = lax.broadcasted_iota(jnp.int32, (tokens, tokens), 1)
     before = jnp.where(r0 < r1, 1.0, 0.0).astype(BF)
@@ -102,24 +114,31 @@
     pr_ref[...] = prob
 
     for j in range(2):
-        for m, start in enumerate((ti, opp)):
-            at = pl.multiple_of(start * PART + j * LANES, LANES)
-            cols = slice(m * LANES, (m + 1) * LANES)
-            rhs_ref[j * tokens : (j + 1) * tokens, cols] = tok_ref[:, pl.ds(at, LANES)]
-            rhs_ref[(2 + j) * tokens : (3 + j) * tokens, cols] = cot_ref[:, pl.ds(at, LANES)]
-
-    def send_copy(c, s):
+        for u in range(nt):
+            cols = slice(u * LANES, (u + 1) * LANES)
+            at = slice(u * PART + j * LANES, u * PART + (j + 1) * LANES)
+            all_ref[j * tokens : (j + 1) * tokens, cols] = tok_ref[:, at]
+            all_ref[(2 + j) * tokens : (3 + j) * tokens, cols] = cot_ref[:, at]
+    for m, start in enumerate((ti, opp)):
+        at = pl.ds(pl.multiple_of(start * LANES, LANES), LANES)
+        rhs_ref[:, m * LANES : (m + 1) * LANES] = all_ref[:, at]
+
+    def send_copy(c, s, near):
         to = peer_to(c, s)
+        src, dst, first = (nsend_ref, nrecv_ref, ring) if near else (send_ref, recv_ref, 0)
+        row = (c - first) * wide
         return pltpu.make_async_remote_copy(
-            src_ref=send_ref.at[pl.ds(pl.multiple_of(to * OUT, OUT), OUT)],
-            dst_ref=recv_ref.at[pl.ds(pl.multiple_of((c * wide + s) * OUT, OUT), OUT)],
-            send_sem=a2a_s,
+            src_ref=src.at[
+                pl.ds(pl.multiple_of((row + to - row_to(c) * wide) * OUT, OUT), OUT)
+            ],
+            dst_ref=dst.at[pl.ds(pl.multiple_of((row + s) * OUT, OUT), OUT)],
+            send_sem=near_s if near else a2a_s,
             recv_sem=a2a_r.at[c],
             device_id=(to, ti),
             device_id_type=MESH,
         )
 
-    def pack(c):
+    def select(c):
         first = row_to(c) * wide
         keys = key_ref[pl.ds(pl.multiple_of(first, wide), wide), :]
         probs = pr_ref[pl.ds(pl.multiple_of(first, wide), wide), :]
@@ -132,28 +151,44 @@
                 sel_ref[i * OUT : (i + 1) * OUT, j * tokens : (j + 1) * tokens] = jnp.where(
                     place - float(CAP * j) == key, value, 0.0
                 ).astype(BF)
-        at = pl.ds(pl.multiple_of(first * OUT, OUT), wide * OUT)
-        send_ref[at, :] = dot(sel_ref[...], rhs_ref[...]).astype(BF)
+
+    def far_rows(c):
+        return pl.ds(pl.multiple_of(c * wide * OUT, OUT), wide * OUT)
+
+    def pack(c):
+        select(c)
+        if isinstance(c, int) and c >= ring:
+            nsend_ref[far_rows(c - ring), :] = dot(sel_ref[...], all_ref[...]).astype(BF)
+        else:
+            send_ref[far_rows(c), :] = dot(sel_ref[...], rhs_ref[...]).astype(BF)
+
+    def send(chunks):
+        for c in chunks:
+            pack(c)
+        for i in range(wide):
+            for c in chunks:
+                send_copy(c, turned(i), c >= ring).start()
+
+    groups = [range(c, min(c + 2, ring)) for c in range(1, ring, 2)] + [range(ring, ny)]
 
     pack(0)
+    mine = ei - yy * wide
     own = pltpu.make_async_copy(
-        send_ref.at[pl.ds(pl.multiple_of(ei * OUT, OUT), OUT)],
+        send_ref.at[pl.ds(pl.multiple_of(mine * OUT, OUT), OUT)],
         recv_ref.at[pl.ds(0, OUT)],
         a2a_r.at[0],
     )
     own.start()
     pl.semaphore_wait(bar, ne + 1)
     for s in range(1, wide):
-        send_copy(0, s).start()
-
-    @pl.loop(1, ny)
-    def _(c):
-        pack(c)
-        for s in range(wide):
-            send_copy(c, s).start()
-
-    w_ref[:, :LANES] = wg_ref[...]
-    w_ref[:, LANES:] = wu_ref[...]
+        send_copy(0, s, False).start()
+
+    for group in groups[:AHEAD]:
+        send(group)
+
+    def prepare():
+        w_ref[:, :LANES] = wg_ref[...]
+        w_ref[:, LANES:] = wu_ref[...]
 
     def block(c):
         return pl.ds(pl.multiple_of(c * rows, rows), rows)
@@ -184,6 +219,21 @@
         for way in range(2):
             ag_copy(c, 0, way).start()
 
+    def direct(c):
+        got = nrecv_ref.at[far_rows(c - ring)]
+        pltpu.make_async_copy(got, got, a2a_r.at[c]).wait()
+        for g in range(wide // gp):
+            at = pl.multiple_of(((c - ring) * wide + g * gp) * OUT, OUT)
+            to = pl.ds(pl.multiple_of(c * rows + g * gp * CAP, gp * CAP), gp * CAP)
+            for u in range(0, nt, 2):
+                cols = slice(u * LANES, (u + 2) * LANES)
+                out = dot(perm_ref[...], nrecv_ref[pl.ds(at, gp * OUT), cols]).astype(BF)
+                for j in range(4):
+                    piece = out[j * gp * CAP : (j + 1) * gp * CAP, :]
+                    g_ref[u, to, j * LANES : (j + 1) * LANES] = piece[:, :LANES]
+                    g_ref[u + 1, to, j * LANES : (j + 1) * LANES] = piece[:, LANES:]
+        hidden(c)
+
     def ag_wait(c, s):
         for way in range(2):
             unit = lax.rem(ti + nt - s - 1, nt) if way == 0 else lax.rem(ti + s + 1, nt)
@@ -221,6 +271,9 @@
 
     def middle(c):
         ag_wait(c, half - 2)
+        hidden(c)
+
+    def hidden(c):
         at = block(c)
         both = jnp.zeros((rows, 2 * LANES), F32)
         dhid = jnp.zeros((rows, LANES), F32)
@@ -284,13 +337,13 @@
                 ret_recv.at[pl.ds(pl.multiple_of(ei * BACK, BACK), BACK)],
                 ret_r.at[c],
             ).start()
+            for s in range(1, wide):
+                back_copy(c, s).start()
 
         @pl.when(c != 0)
         def _():
-            back_copy(c, 0).start()
-
-        for s in range(1, wide):
-            back_copy(c, s).start()
+            for i in range(wide):
+                back_copy(c, turned(i)).start()
 
     def weight_grads(u):
         at = pl.ds(pl.multiple_of(u * PART, PART), PART)
@@ -299,59 +352,86 @@
         gu_ref[at, :] = both[:, LANES:]
         gd_ref[:, at] = t_dot(sc_ref[...], g_ref[u, :, PART:]).astype(BF)
 
-    stages = [arrive]
-    stages += [functools.partial(forward, s) for s in range(1, half - 1)]
-    stages += [middle]
-    stages += [functools.partial(add, k) for k in range(1, half)]
-    stages += [finish]
-
-    hits_n = jnp.zeros((tokens, ne), F32)
-    experts_n = lax.broadcasted_iota(jnp.int32, (tokens, ne), 1)
-    for k in range(ids_ref.shape[1]):
-        hits_n = jnp.where(ids_ref[:, k : k + 1] == experts_n, 1.0, hits_n)
-    after = jnp.where(r1 < r0, 1.0, 0.0).astype(BF)
-    key_n = jnp.where(hits_n > 0.0, dot(after, hits_n.astype(BF)), 200.0).astype(BF)
-    tile = min(ne * BACK, 512)
-    for n in range(0, ne * BACK, tile):
-        want = dot(key_n, expand_ref[:, n : n + tile])
-        phase = phase_ref[:, n : n + tile]
-        lo_ref[:, n : n + tile] = jnp.where(want == phase, 1.0, 0.0).astype(BF)
-        hi_ref[:, n : n + tile] = jnp.where(want + float(CAP) == phase, 1.0, 0.0).astype(BF)
-
-    last = ny + half - 1
-    each = nt // half
-
-    @pl.loop(0, ny + len(stages) - 1)
+    sums = [functools.partial(add, k) for k in range(1, half)] + [finish]
+    stages = [arrive] + [functools.partial(forward, s) for s in range(1, half - 1)]
+    stages += [middle] + sums
+
+    def places():
+        e0 = lax.broadcasted_iota(jnp.int32, (ne, ne), 0)
+        e1 = lax.broadcasted_iota(jnp.int32, (ne, ne), 1)
+        hits_n = t_dot(hits.astype(BF), jnp.where(e0 == e1, 1.0, 0.0).astype(BF))
+        after = jnp.where(r1 < r0, 1.0, 0.0).astype(BF)
+        key_n = jnp.where(hits_n > 0.0, dot(after, hits_n.astype(BF)), 200.0).astype(BF)
+        tile = min(ne * BACK, 512)
+        for n in range(0, ne * BACK, tile):
+            want = dot(key_n, expand_ref[:, n : n + tile])
+            phase = phase_ref[:, n : n + tile]
+            lo_ref[:, n : n + tile] = jnp.where(want == phase, 1.0, 0.0).astype(BF)
+            hi_ref[:, n : n + tile] = jnp.where(want + float(CAP) == phase, 1.0, 0.0).astype(BF)
+
+    turns = max(ring - 1 + len(stages), ny - 1 + LAG + len(sums) + 1)
+    last = max(ring + half - 1, ny + LAG)
+    each = -(-nt // (turns - last))
+
+    @pl.loop(0, turns)
     def _(turn):
+        for i, group in enumerate(groups[AHEAD:]):
+            pl.when(turn == i)(functools.partial(send, group))
         for i, stage in enumerate(stages):
             c = turn - i
-            pl.when(jnp.logical_and(c >= 0, c < ny))(functools.partial(stage, c))
-
-        @pl.when(turn >= last)
-        def _():
-            for i in range(each):
-                weight_grads((turn - last) * each + i)
-
-    @pl.loop(0, ny)
-    def _(c):
-        got = ret_recv.at[pl.ds(pl.multiple_of(c * wide * BACK, BACK), wide * BACK)]
+            pl.when(jnp.logical_and(c >= 0, c < ring))(functools.partial(stage, c))
+            if i == 0:
+                pl.when(turn == 0)(prepare)
+                pl.when(turn == 1)(places)
+        for i, stage in enumerate([direct] + sums):
+            c = turn - i - LAG
+            pl.when(jnp.logical_and(c >= ring, c < ny))(functools.partial(stage, c))
+        for i in range(each):
+            u = (turn - last) * each + i
+            pl.when(jnp.logical_and(turn >= last, u < nt))(functools.partial(weight_grads, u))
+
+    low = jnp.zeros((tokens, LANES), F32)
+    high = jnp.zeros((tokens, LANES), F32)
+    for c in range(ny):
+        at = pl.ds(pl.multiple_of(row_to(c) * wide * BACK, wide * BACK), wide * BACK)
+        got = ret_recv.at[at]
         pltpu.make_async_copy(got, got, ret_r.at[c]).wait()
-
-    gi_ref[:, :LANES] = dot(lo_ref[...], ret_recv[...]).astype(BF)
-    gi_ref[:, LANES:] = dot(hi_ref[...], ret_recv[...]).astype(BF)
-
-    sent = send_ref.at[pl.ds(0, (ne - 1) * OUT)]
+        low = low + dot(lo_ref[:, at], ret_recv[at, :])
+        high = high + dot(hi_ref[:, at], ret_recv[at, :])
+    gi_ref[:, :LANES] = low.astype(BF)
+    gi_ref[:, LANES:] = high.astype(BF)
+
+    sent = send_ref.at[pl.ds(0, (ring * wide - 1) * OUT)]
     pltpu.make_async_copy(sent, sent, a2a_s).wait()
+    pltpu.make_async_copy(nsend_ref, nsend_ref, near_s).wait()
     sent = ret_send.at[pl.ds(0, (ne - 1) * BACK)]
     pltpu.make_async_copy(sent, sent, ret_s).wait()
     for way in range(2):
         for s in range(half - 1):
-            pltpu.make_async_copy(g_ref.at[0], g_ref.at[0], ag_s.at[way, s]).wait()
+            sent = g_ref.at[0, pl.ds(0, ring * rows)]
+            pltpu.make_async_copy(sent, sent, ag_s.at[way, s]).wait()
         for k in range(half):
             sent = rs_send.at[0, 0]
             if k == 0:
                 sent = rs_send.at[0, 0, pl.ds(0, ny * (rows // 2))]
             pltpu.make_async_copy(sent, sent, rs_s.at[way, k]).wait()
+
+
+def settle(*arrays):
+    n = len(arrays)
+
+    def body(*refs):
+        for i in range(n):
+            refs[n + i][...] = refs[i][...]
+
+    vmem = pl.BlockSpec(memory_space=pltpu.VMEM)
+    return pl.pallas_call(
+        body,
+        out_shape=tuple(jax.ShapeDtypeStruct(a.shape, a.dtype) for a in arrays),
+        in_specs=[vmem] * n,
+        out_specs=(vmem,) * n,
+        compiler_params=pltpu.CompilerParams(vmem_limit_bytes=16 * 1024 * 1024),
+    )(*arrays)
 
 
 def tables(ne, side):
@@ -379,6 +459,8 @@
     wide = 2 * side
     ny, half = ne // wide, nt // 2
     rows = ne * CAP
+    ring = ring_chunks(ny)
+    direct = ny - ring
     gp, perm, back, expand, phase = tables(ne, side)
 
     def step(tokens, cotangent, expert_ids, gate_probs, w_gate, w_up, w_down):
@@ -393,15 +475,18 @@
                 jax.ShapeDtypeStruct((width, LANES), BF),
                 jax.ShapeDtypeStruct((LANES, width), BF),
             ),
-            in_specs=[vmem] * 12,
+            in_specs=[vmem] * 11,
             out_specs=(vmem,) * 4,
             scratch_shapes=[
                 pltpu.VMEM((ne, owned), F32),
                 pltpu.VMEM((ne, owned), F32),
                 pltpu.VMEM((4 * owned, 2 * LANES), BF),
+                pltpu.VMEM((4 * owned, nt * LANES), BF),
                 pltpu.VMEM((wide * OUT, 4 * owned), BF),
-                pltpu.VMEM((ne * OUT, 2 * LANES), BF),
-                pltpu.VMEM((ne * OUT, 2 * LANES), BF),
+                pltpu.VMEM((ring * wide * OUT, 2 * LANES), BF),
+                pltpu.VMEM((ring * wide * OUT, 2 * LANES), BF),
+                pltpu.VMEM((direct * wide * OUT, nt * LANES), BF),
+                pltpu.VMEM((direct * wide * OUT, nt * LANES), BF),
                 pltpu.VMEM((nt, rows, 2 * PART), BF),
                 pltpu.VMEM((width, 2 * LANES), BF),
                 pltpu.VMEM((rows, 2 * LANES), BF),
@@ -413,9 +498,10 @@
                 pltpu.VMEM((owned, ne * BACK), BF),
                 pltpu.VMEM((owned, ne * BACK), BF),
                 dma,
+                dma,
                 dma((ny,)),
                 dma((2, half - 1)),
-                dma((2, half - 1, ny)),
+                dma((2, half - 1, ring)),
                 dma((2, half)),
                 dma((2, half, ny)),
                 dma,
@@ -425,9 +511,8 @@
                 collective_id=0, has_side_effects=True, vmem_limit_bytes=56 * 1024 * 1024
             ),
         )(
-            expert_ids,
             expert_ids.T,
-            gate_probs.T.astype(F32),
+            gate_probs.T,
             tokens,
             cotangent,
             w_gate[0],
@@ -438,6 +523,7 @@
             jnp.asarray(expand),
             jnp.asarray(phase),
         )
+        gi, gg, gu, gd = settle(gi, gg, gu, gd)
         return gi, gg[None], gu[None], gd[None]
 
     return jax.shard_map(

time: 190 us -> 172 us (0.905); the launches traced: 190 us -> 169 us
  Pallas kernels: 182 us -> 164 us
  local copies, waits for them, and re-layouts: 6.82 us -> 3.96 us
    pallas_call x1, Pallas kernels: 182 us -> 163 us  [step(): pl.pallas_call(functools.partial(kernel, ne, nt, side, gp), out_shape=(ja...]
    unnamed x13 -> x8, local copies, waits for them, and re-layouts: 6.82 us -> 3.96 us
where the time goes in v2:
time: 172 us; the launch traced here: 169 us
  Pallas kernels  164 us (95%)
  local copies, waits for them, and re-layouts  3.96 us (2%)
    pallas_call x1, Pallas kernels, step(): pl.pallas_call(functools.partial(kernel, ne, nt, side, gp), out_shape=(ja...  163 us
    unnamed x8, local copies, waits for them, and re-layouts  3.96 us

profile of v2, /device:TPU:1, one launch (start us, length us, event | category | flops | bytes accessed | tf_op | source)
XLA Modules:
  0.0 168.7 jit_solution(4140790432365796479)
XLA Ops:
  0.6 162.8 %shard_map.138 = (bf16[128,256]{1,0:T(8,128)(2,1)}, bf16[2048,128]{1,0:T(8,128)(2,1)}, bf16[2048,128]{1,0:T(8,128)(2,1)}, bf16[128,2048]{1,0:T(8,128)(2,1)}) custom-call(s32[8,128]{1,0:T(8,128)} %bitcast.11, bf16[8,128]{1,0:T(8,128)(2,1)} %bitcast.12, bf16[128,2048]{1,0:T(8,128)(2,1)} %tok_ref.1, bf16[128,2048]{1,0:T(8,128)(2,1)} %cot_ref.1, ...), custom_call_target="tpu_custom_call" | custom-call | tf_op jit(solution)/shard_map/pallas_call | solution.py:470
  163.5 0.0 copy-start
  163.5 1.0 copy-done
  164.5 0.0 copy-start.1
  164.5 1.0 copy-done.1
  165.5 0.0 copy-start.2
  165.5 1.0 copy-done.2
  166.6 0.0 copy-start.3
  166.6 0.8 copy-done.3
  167.4 1.3 shard_map.139
Async XLA Ops:
  163.5 1.0 copy-start
  164.5 1.0 copy-start.1
  165.5 1.0 copy-start.2
  166.6 0.8 copy-start.3

commit v3 on v2

--- a/solution.py
+++ b/solution.py
@@ -40,12 +40,12 @@
 
 def kernel(
     ne, nt, side, gp,
-    idst_ref, probst_ref, tok_ref, cot_ref, wg_ref, wu_ref, wd_ref,
-    perm_ref, back_ref, expand_ref, phase_ref,
+    idst_ref, probst_ref, tok_ref, cot_ref, wg_hbm, wu_hbm, wd_hbm,
+    perm_ref, back_hbm, expand_hbm, phase_ref,
     gi_ref, gg_ref, gu_ref, gd_ref,
-    key_ref, pr_ref, rhs_ref, all_ref, sel_ref, send_ref, recv_ref, nsend_ref, nrecv_ref, g_ref, w_ref, d_ref, sc_ref,
+    wd_ref, back_ref, expand_ref, key_ref, pr_ref, rhs_ref, all_ref, sel_ref, send_ref, recv_ref, nsend_ref, nrecv_ref, g_ref, w_ref, d_ref, sc_ref,
     rs_send, rs_recv, ret_send, ret_recv, lo_ref, hi_ref,
-    a2a_s, near_s, a2a_r, ag_s, ag_r, rs_s, rs_r, ret_s, ret_r,
+    a2a_s, near_s, a2a_r, ag_s, ag_r, rs_s, rs_r, ret_s, ret_r, load_s,
 ):
     wide = 2 * side
     ny = ne // wide
@@ -89,6 +89,19 @@
         def _(c):
             for s in range(wide):
                 act(c, s)
+
+    loads = [
+        pltpu.make_async_copy(src, dst, load_s.at[i])
+        for i, (src, dst) in enumerate(
+            (
+                (wg_hbm, w_ref.at[:, pl.ds(0, LANES)]),
+                (wu_hbm, w_ref.at[:, pl.ds(LANES, LANES)]),
+                (wd_hbm, wd_ref),
+                (back_hbm, back_ref),
+                (expand_hbm, expand_ref),
+            )
+        )
+    ]
 
     bar = pltpu.get_barrier_semaphore()
     others(
@@ -114,14 +127,11 @@
     pr_ref[...] = prob
 
     for j in range(2):
-        for u in range(nt):
-            cols = slice(u * LANES, (u + 1) * LANES)
-            at = slice(u * PART + j * LANES, u * PART + (j + 1) * LANES)
-            all_ref[j * tokens : (j + 1) * tokens, cols] = tok_ref[:, at]
-            all_ref[(2 + j) * tokens : (3 + j) * tokens, cols] = cot_ref[:, at]
-    for m, start in enumerate((ti, opp)):
-        at = pl.ds(pl.multiple_of(start * LANES, LANES), LANES)
-        rhs_ref[:, m * LANES : (m + 1) * LANES] = all_ref[:, at]
+        for m, start in enumerate((ti, opp)):
+            at = pl.ds(pl.multiple_of(start * PART + j * LANES, LANES), LANES)
+            cols = slice(m * LANES, (m + 1) * LANES)
+            rhs_ref[j * tokens : (j + 1) * tokens, cols] = tok_ref[:, at]
+            rhs_ref[(2 + j) * tokens : (3 + j) * tokens, cols] = cot_ref[:, at]
 
     def send_copy(c, s, near):
         to = peer_to(c, s)
@@ -183,12 +193,20 @@
     for s in range(1, wide):
         send_copy(0, s, False).start()
 
+    for load in loads:
+        load.start()
     for group in groups[:AHEAD]:
         send(group)
+    for j in range(2):
+        for u in range(nt):
+            cols = slice(u * LANES, (u + 1) * LANES)
+            at = slice(u * PART + j * LANES, u * PART + (j + 1) * LANES)
+            all_ref[j * tokens : (j + 1) * tokens, cols] = tok_ref[:, at]
+            all_ref[(2 + j) * tokens : (3 + j) * tokens, cols] = cot_ref[:, at]
 
     def prepare():
-        w_ref[:, :LANES] = wg_ref[...]
-        w_ref[:, LANES:] = wu_ref[...]
+        for load in loads:
+            load.wait()
 
     def block(c):
         return pl.ds(pl.multiple_of(c * rows, rows), rows)
@@ -421,16 +439,26 @@
     n = len(arrays)
 
     def body(*refs):
+        here, sems = refs[2 * n : 3 * n], refs[3 * n]
+        ins = [pltpu.make_async_copy(refs[i], here[i], sems.at[0, i]) for i in range(n)]
+        outs = [pltpu.make_async_copy(here[i], refs[n + i], sems.at[1, i]) for i in range(n)]
+        for copy in ins:
+            copy.start()
         for i in range(n):
-            refs[n + i][...] = refs[i][...]
-
-    vmem = pl.BlockSpec(memory_space=pltpu.VMEM)
+            ins[i].wait()
+            outs[i].start()
+        for copy in outs:
+            copy.wait()
+
+    any_space = pl.BlockSpec(memory_space=pl.ANY)
     return pl.pallas_call(
         body,
         out_shape=tuple(jax.ShapeDtypeStruct(a.shape, a.dtype) for a in arrays),
-        in_specs=[vmem] * n,
-        out_specs=(vmem,) * n,
-        compiler_params=pltpu.CompilerParams(vmem_limit_bytes=16 * 1024 * 1024),
+        in_specs=[any_space] * n,
+        out_specs=(any_space,) * n,
+        scratch_shapes=[pltpu.VMEM(a.shape, a.dtype) for a in arrays]
+        + [pltpu.SemaphoreType.DMA((2, n))],
+        compiler_params=pltpu.CompilerParams(vmem_limit_bytes=56 * 1024 * 1024),
     )(*arrays)
 
 
@@ -466,6 +494,7 @@
     def step(tokens, cotangent, expert_ids, gate_probs, w_gate, w_up, w_down):
         owned, width = tokens.shape
         vmem = pl.BlockSpec(memory_space=pltpu.VMEM)
+        hbm = pl.BlockSpec(memory_space=pl.ANY)
         dma = pltpu.SemaphoreType.DMA
         gi, gg, gu, gd = pl.pallas_call(
             functools.partial(kernel, ne, nt, side, gp),
@@ -475,9 +504,12 @@
                 jax.ShapeDtypeStruct((width, LANES), BF),
                 jax.ShapeDtypeStruct((LANES, width), BF),
             ),
-            in_specs=[vmem] * 11,
+            in_specs=[vmem] * 4 + [hbm] * 3 + [vmem] + [hbm] * 2 + [vmem],
             out_specs=(vmem,) * 4,
             scratch_shapes=[
+                pltpu.VMEM((LANES, width), BF),
+                pltpu.VMEM(back.shape, BF),
+                pltpu.VMEM(expand.shape, BF),
                 pltpu.VMEM((ne, owned), F32),
                 pltpu.VMEM((ne, owned), F32),
                 pltpu.VMEM((4 * owned, 2 * LANES), BF),
@@ -506,6 +538,7 @@
                 dma((2, half, ny)),
                 dma,
                 dma((ny,)),
+                dma((5,)),
             ],
             compiler_params=pltpu.CompilerParams(
                 collective_id=0, has_side_effects=True, vmem_limit_bytes=56 * 1024 * 1024

time: 172 us -> 168 us (0.977)
  local copies, waits for them, and re-layouts: 3.96 us -> 0 us
    unnamed x8 -> x0, local copies, waits for them, and re-layouts: 3.96 us -> none
where the time goes in v3:
time: 168 us; the launch traced here: 165 us
  Pallas kernels  164 us (98%)
    pallas_call x1, Pallas kernels, step(): pl.pallas_call(functools.partial(kernel, ne, nt, side, gp), out_shape=(ja...  162 us

profile of v3, /device:TPU:1, one launch (start us, length us, event | category | flops | bytes accessed | tf_op | source)
XLA Modules:
  0.0 165.1 jit_solution(17232313623760007924)
XLA Ops:
  0.6 162.2 %shard_map.138 = (bf16[128,256]{1,0:T(8,128)(2,1)}, bf16[2048,128]{1,0:T(8,128)(2,1)}, bf16[2048,128]{1,0:T(8,128)(2,1)}, bf16[128,2048]{1,0:T(8,128)(2,1)}) custom-call(s32[8,128]{1,0:T(8,128)} %bitcast.11, bf16[8,128]{1,0:T(8,128)(2,1)} %bitcast.12, bf16[128,2048]{1,0:T(8,128)(2,1)} %tok_ref.1, bf16[128,2048]{1,0:T(8,128)(2,1)} %cot_ref.1, ...), custom_call_target="tpu_custom_call" | custom-call | tf_op jit(solution)/shard_map/pallas_call | solution.py:499
  162.8 2.3 %shard_map.139 = (bf16[128,256]{1,0:T(8,128)(2,1)}, bf16[2048,128]{1,0:T(8,128)(2,1)}, bf16[2048,128]{1,0:T(8,128)(2,1)}, bf16[128,2048]{1,0:T(8,128)(2,1)}) custom-call(bf16[128,256]{1,0:T(8,128)(2,1)} %get-tuple-element.12.refs_0_, bf16[2048,128]{1,0:T(8,128)(2,1)} %get-tuple-element.13.refs_1_, bf16[2048,128]{1,0:T(8,128)(2,1)} %get-tuple-element.14.refs_2_, ...), custom_call_target="tpu_custom_call" | custom-call | tf_op jit(solution)/shard_map/pallas_call | solution.py:454

commit v4 on v3

--- a/solution.py
+++ b/solution.py
@@ -393,17 +393,21 @@
 
     @pl.loop(0, turns)
     def _(turn):
-        for i, group in enumerate(groups[AHEAD:]):
-            pl.when(turn == i)(functools.partial(send, group))
-        for i, stage in enumerate(stages):
+        for i, stage in reversed(list(enumerate(stages))[1:]):
             c = turn - i
             pl.when(jnp.logical_and(c >= 0, c < ring))(functools.partial(stage, c))
-            if i == 0:
-                pl.when(turn == 0)(prepare)
-                pl.when(turn == 1)(places)
-        for i, stage in enumerate([direct] + sums):
+        for i, stage in reversed(list(enumerate([direct] + sums))):
             c = turn - i - LAG
             pl.when(jnp.logical_and(c >= ring, c < ny))(functools.partial(stage, c))
+        pl.when(turn < ring)(functools.partial(arrive, turn))
+
+        @pl.when(turn == 0)
+        def _():
+            for group in groups[AHEAD:]:
+                send(group)
+            prepare()
+            places()
+
         for i in range(each):
             u = (turn - last) * each + i
             pl.when(jnp.logical_and(turn >= last, u < nt))(functools.partial(weight_grads, u))

time: 168 us -> 163 us (0.970); the launches traced: 165 us -> 162 us
  Pallas kernels: 164 us -> 162 us
    pallas_call x1, Pallas kernels: 162 us -> 159 us  [step(): pl.pallas_call(functools.partial(kernel, ne, nt, side, gp), out_shape=(ja...]
where the time goes in v4:
time: 163 us; the launch traced here: 162 us
  Pallas kernels  162 us (99%)
    pallas_call x1, Pallas kernels, step(): pl.pallas_call(functools.partial(kernel, ne, nt, side, gp), out_shape=(ja...  159 us

profile of v4, /device:TPU:1, one launch (start us, length us, event | category | flops | bytes accessed | tf_op | source)
XLA Modules:
  0.0 162.4 jit_solution(14941488462854953245)
XLA Ops:
  0.6 159.4 %shard_map.138 = (bf16[128,256]{1,0:T(8,128)(2,1)}, bf16[2048,128]{1,0:T(8,128)(2,1)}, bf16[2048,128]{1,0:T(8,128)(2,1)}, bf16[128,2048]{1,0:T(8,128)(2,1)}) custom-call(s32[8,128]{1,0:T(8,128)} %bitcast.11, bf16[8,128]{1,0:T(8,128)(2,1)} %bitcast.12, bf16[128,2048]{1,0:T(8,128)(2,1)} %tok_ref.1, bf16[128,2048]{1,0:T(8,128)(2,1)} %cot_ref.1, ...), custom_call_target="tpu_custom_call" | custom-call | tf_op jit(solution)/shard_map/pallas_call | solution.py:503
  160.1 2.3 %shard_map.139 = (bf16[128,256]{1,0:T(8,128)(2,1)}, bf16[2048,128]{1,0:T(8,128)(2,1)}, bf16[2048,128]{1,0:T(8,128)(2,1)}, bf16[128,2048]{1,0:T(8,128)(2,1)}) custom-call(bf16[128,256]{1,0:T(8,128)(2,1)} %get-tuple-element.12.refs_0_, bf16[2048,128]{1,0:T(8,128)(2,1)} %get-tuple-element.13.refs_1_, bf16[2048,128]{1,0:T(8,128)(2,1)} %get-tuple-element.14.refs_2_, ...), custom_call_target="tpu_custom_call" | custom-call | tf_op jit(solution)/shard_map/pallas_call | solution.py:458
